TPU v7x, 32 devices: a whole 2x2x4 slice. The times are simulated.
32 devices in a mesh: tok: 4 (over y, x), vocab: 8 (over z, core).
Axes of the slice: x: 2, y: 2, z: 4, core: 2. Of those that a mesh axis runs over, the one named last changes fastest.
Arguments:
- teacher_logits: bfloat16 [512, 32768], P('tok', 'vocab'), may hold values from -18 to 240
- hidden: bfloat16 [512, 4608], P('tok'), may hold values from -6 to 6
- new_head: bfloat16 [4608, 32768], P(None, ('tok', 'vocab')), may hold values from -0.26516504 to 0.26516504
- labels: int32 [512], replicated, may hold values from 0 to 32767
- map_target: int32 [256, 4], P('vocab'), may hold values from 0 to 255, as said below
- map_weight: bfloat16 [256, 4, 128, 128], P('vocab'), may hold values from 0 to 0.017578125, as said below
Outputs:
- loss: float32 [512], P('tok')
- head_grad: bfloat16 [4608, 32768], P(None, ('tok', 'vocab'))
Inputs may be any that keep to these rules, and one draw needn't show every extreme that they name: `map_target`: values are ids of new blocks; new block b belongs to the device at index b // 8 of tok and vocab together, tok first. Of the 128 entries of one vocab index, at most 8 belong to one device, and some device gets exactly 8. `map_weight`: entries are non-negative.
All inputs are finite; a program needn't handle non-finite values.
Results may differ from a plain program's by a relative error of at most 0.001.
The roundings to bfloat16 on the way count: a program that leaves them out, or rounds other values in their place, can miss the bound.
Values may be sent and summed in bfloat16 or wider, within the bound.
No kernel may reach another device: no remote copies, remote signals or barrier semaphores. Data moves between devices by JAX's collectives and lax.ppermute only.
A program may use at most 128 MiB of HBM per device.

v0:
```python
import jax
import jax.numpy as jnp
from jax import lax
from jax.sharding import PartitionSpec as P


def local(teacher_logits, hidden, new_head, labels, map_target, map_weight):
    tok_rows = teacher_logits.shape[0]
    block = map_weight.shape[2]
    fanout = map_weight.shape[1]
    old_blocks = map_target.shape[0]
    entries = old_blocks * fanout
    n_tok = lax.axis_size("tok")
    n_vocab = lax.axis_size("vocab")
    nodes = n_tok * n_vocab
    capacity = max(2, 2 * entries // nodes)
    new_cols = new_head.shape[1]
    per_node = new_cols // block
    own_index = lax.axis_index(("tok", "vocab"))
    scores = teacher_logits.astype(jnp.float32)
    local_top = jnp.max(scores, axis=1)
    highest = lax.pmax(local_top, "vocab")
    total = lax.psum(jnp.sum(jnp.exp(scores - highest[:, None]), axis=1), "vocab")
    teacher_prob = (jnp.exp(scores - highest[:, None]) / total[:, None]).astype(jnp.bfloat16)
    pieces = teacher_prob.reshape(tok_rows, old_blocks, block)
    contrib = jnp.einsum("tjb,jkbc->jktc", pieces, map_weight, preferred_element_type=jnp.float32)
    contrib = contrib.astype(jnp.bfloat16).reshape(entries, tok_rows, block)
    owners = (map_target // per_node).reshape(entries)
    earlier = jnp.arange(entries)[None, :] < jnp.arange(entries)[:, None]
    slots = jnp.sum((owners[:, None] == owners[None, :]) & earlier, axis=1)
    outbox = (
        jnp.zeros((nodes, capacity, tok_rows, block), jnp.bfloat16).at[owners, slots].set(contrib)
    )
    inbox = lax.all_to_all(outbox, ("tok", "vocab"), split_axis=0, concat_axis=0, tiled=True)
    inbox = inbox.reshape(n_tok, n_vocab, capacity, tok_rows, block)
    targets_all = lax.all_gather(map_target, "vocab", axis=0, tiled=True).reshape(n_vocab, entries)
    owners_all = targets_all // per_node
    local_block = targets_all % per_node
    slots_all = jnp.sum((owners_all[:, :, None] == owners_all[:, None, :]) & earlier[None], axis=2)
    picked = (owners_all == own_index)[:, :, None] & (
        slots_all[:, :, None] == jnp.arange(capacity)[None, None, :]
    )
    block_hit = local_block[:, :, None] == jnp.arange(per_node)[None, None, :]
    landing = jnp.einsum(
        "vec,veb->vcb", picked.astype(jnp.float32), block_hit.astype(jnp.float32)
    ).astype(jnp.bfloat16)
    target = jnp.einsum("vcb,svctk->stbk", landing, inbox, preferred_element_type=jnp.float32)
    target = target.reshape(n_tok * tok_rows, new_cols)
    everyone = lax.all_gather(hidden, "tok", axis=0, tiled=True)
    logits = jnp.dot(everyone, new_head, preferred_element_type=jnp.float32)
    columns = own_index * new_cols + jnp.arange(new_cols, dtype=jnp.int32)
    label_hit = labels[:, None] == columns[None, :]
    label_part = jnp.sum(jnp.where(label_hit, logits, 0.0), axis=1)
    mass_part = jnp.sum(target, axis=1)
    inner_part = jnp.sum(target * logits, axis=1)
    row_top = jnp.max(logits, axis=1)
    top_all = lax.pmax(row_top, ("tok", "vocab"))
    exp_part = jnp.sum(jnp.exp(logits - top_all[:, None]), axis=1)
    total_all, target_mass, inner, label_logit = lax.psum(
        (exp_part, mass_part, inner_part, label_part), ("tok", "vocab")
    )
    log_total = top_all + jnp.log(total_all)
    loss_all = target_mass * log_total - inner + log_total - label_logit
    loss = lax.dynamic_slice_in_dim(loss_all, lax.axis_index("tok") * tok_rows, tok_rows)
    probs = jnp.exp(logits - log_total[:, None])
    grad_logits = (
        (target_mass + 1.0)[:, None] * probs - target - label_hit.astype(jnp.float32)
    ).astype(jnp.bfloat16)
    head_grad = lax.dot_general(
        everyone, grad_logits, (((0,), (0,)), ((), ())), preferred_element_type=jnp.float32
    )
    return (loss, head_grad.astype(jnp.bfloat16))


def solution(mesh):
    return jax.shard_map(
        local,
        mesh=mesh,
        in_specs=(
            P("tok", "vocab"),
            P("tok", None),
            P(None, ("tok", "vocab")),
            P(),
            P("vocab", None),
            P("vocab", None, None, None),
        ),
        out_specs=(P("tok"), P(None, ("tok", "vocab"))),
        check_vma=False,
    )
```

profile of v0, /device:TPU:0, one launch (start us, length us, event | category | flops | bytes accessed | tf_op | source)
XLA Modules:
  0.0 402.5 jit_solution(13277230219794109797)
XLA Ops:
  7.2 0.0 copy-start
  7.2 0.8 add_select_fusion.2
  8.0 0.1 copy.44
  8.0 0.1 eq.79
  8.2 0.1 reshape.176
  8.3 1.5 reduce_max.23
  9.7 18.1 %pmax.14 = f32[128]{0:T(128)S(1)} all-reduce(bf16[128]{0:T(256)(128)(2,1)S(1)} %reduce_max.23), channel_id=1, replica_groups=mesh['tok'=4,'vocab'=8] {'vocab'}, use_global_device_ids=true, to_apply=%region_2.0 | all-reduce | flops 128 | bytes 768 | tf_op jit(solution)/shard_map/pmax | solution.py:22
  27.8 1.7 fusion.7
  29.5 13.6 %psum.35 = f32[128]{0:T(128)S(1)} all-reduce(f32[128]{0:T(128)S(1)} %fusion.7), channel_id=1, replica_groups=mesh['tok'=4,'vocab'=8] {'vocab'}, use_global_device_ids=true, to_apply=%region_4.5 | all-reduce | flops 128 | bytes 1024 | tf_op jit(solution)/shard_map/psum | solution.py:23
  43.1 0.5 fusion.9
  43.6 0.2 copy.61
  43.8 0.2 convert_reduce_fusion.1
  44.0 1.3 copy-done.1
  45.3 3.2 convolution_convert_fusion.1
  48.5 5.5 %broadcast_in_dim.5 = bf16[32,8,128,128]{3,2,1,0:T(8,128)(2,1)} broadcast(bf16[]{:T(256)} %constant.49.clone.1), dimensions={} | broadcast | bytes 8388610 | tf_op jit(solution)/shard_map/broadcast_in_dim | solution.py:32
  54.0 20.7 %scatter_fusion = bf16[32,8,128,128]{3,2,1,0:T(8,128)(2,1)} fusion(bf16[32,8,128,128]{3,2,1,0:T(8,128)(2,1)} %broadcast_in_dim.5, s32[128]{0:T(128)S(1)} %fusion.30, bf16[128,128,128]{2,1,0:T(8,128)(2,1)} %bitcast.47), kind=kCustom, calls=%fused_computation | custom fusion | bytes 12583936 | tf_op jit(solution)/shard_map/scatter | solution.py:32
  74.7 3.8 all-to-all-start
  78.6 0.0 all-gather.3.cloned.1.call-start
  78.6 0.7 all-gather.3.cloned.1.call-update
  79.3 188.6 %all-gather = s32[8,32,4]{1,2,0:T(4,128)S(1)} all-gather(s32[1,32,4]{1,2,0:T(4,128)S(1)} %bitcast.50), channel_id=1, replica_groups=mesh['tok'=4,'vocab'=8] {'vocab'}, dimensions={0}, use_global_device_ids=true | all-gather | bytes 4608 | tf_op jit(solution)/shard_map/all_gather | solution.py:36
  267.9 0.1 copy.47
  268.1 0.4 convert_reduce_fusion
  268.5 0.0 all-gather.3.cloned.1.call-done
  268.5 10.1 %fusion.31 = (f32[512]{0:T(512)S(1)}, f32[512,1024]{1,0:T(8,128)}) fusion(bf16[512,4608]{1,0:T(8,128)(2,1)} %all-gather.3.cloned.1.call-done, bf16[4608,1024]{1,0:T(8,128)(2,1)} %param.8), kind=kOutput, calls=%fused_computation.63 | convolution fusion | flops 4832361984 | bytes 16254976 | tf_op jit(solution)/shard_map/dot_general | solution.py:50
  278.6 38.1 %pmax.15 = f32[512]{0:T(512)S(1)} all-reduce(f32[512]{0:T(512)S(1)} %get-tuple-element.24), channel_id=1, replica_groups=mesh['tok'=4,'vocab'=8] {'tok','vocab'}, use_global_device_ids=true, to_apply=%region_10.11 | all-reduce | flops 512 | bytes 4096 | tf_op jit(solution)/shard_map/pmax | solution.py:57
  316.7 0.0 all-to-all-done
  316.7 10.5 %bitcast_reduce_fusion = (f32[4,128]{1,0:T(4,128)S(1)}, f32[4,128,128,8,1]{2,3,4,1,0:T(8,128)S(1)}) fusion(s32[8,128]{1,0:T(8,128)S(1)} %add_select_fusion, s32[8,128]{1,0:T(8,128)S(1)} %convert_reduce_fusion, pred[8,128]{1,0:T(8,128)(4,1)S(1)} %get-tuple-element.21, bf16[4,8,8,128,128]{4,3,2,1,0:T(8,128)(2,1)} %bitcast.5), kind=kOutput, calls=%fused_computation.14 | convolution fusion | flops 67788800 | bytes 10497024 | tf_op jit(solution)/shard_map/vcb,svctk->stbk/dot_general | solution.py:47
  327.2 2.8 fusion.6
  330.0 41.5 %all-reduce = (f32[512]{0:T(512)S(1)}, f32[512]{0:T(512)S(1)}, f32[512]{0:T(512)S(1)}, f32[512]{0:T(512)S(1)}) all-reduce(f32[512]{0:T(512)S(1)} %get-tuple-element.13, f32[512]{0:T(512)S(1)} %get-tuple-element.14, f32[512]{0:T(512)S(1)} %get-tuple-element.12, f32[512]{0:T(512)S(1)} %bitcast.51), channel_id=1, replica_groups=mesh['tok'=4,'vocab'=8] {'tok','vocab'}, use_global_device_ids=true, to_apply=%region_16.17 | all-reduce | flops 2048 | bytes 16384 | tf_op jit(solution)/shard_map/psum | solution.py:59
  371.5 11.0 %fusion.2 = bf16[4608,1024]{0,1:T(8,128)(2,1)} fusion(bf16[512,4608]{1,0:T(8,128)(2,1)} %all-gather.3.cloned.1.call-done, f32[512,1024]{1,0:T(8,128)} %get-tuple-element.25, f32[64,8,8,128]{3,2,1,0:T(8,128)S(1)} %bitcast.46, f32[512]{0:T(512)S(1)} %get-tuple-element.20, f32[512]{0:T(512)S(1)} %get-tuple-element.23, s32[1024]{0:T(1024)S(1)} %iota_add_fusion, ...), kind=kOutput, calls=%fused_computation.4 | convolution fusion | flops 4840226816 | bytes 18360320 | tf_op jit(solution)/shard_map/dot_general | solution.py:69
  382.4 12.6 %copy.54 = bf16[4608,1024]{1,0:T(8,128)(2,1)} copy(bf16[4608,1024]{0,1:T(8,128)(2,1)} %fusion.2) | data formatting | bytes 18874368
  395.0 0.6 dynamic_slice.3
  (13 shorter events, 0.1 us)
Async XLA Ops:
  7.2 35.9 %copy-start = (bf16[128,4096]{1,0:T(8,128)(2,1)S(1)}, bf16[128,4096]{1,0:T(8,128)(2,1)}, u32[]{:S(2)}) copy-start(bf16[128,4096]{1,0:T(8,128)(2,1)} %param.6) | copy-start | bytes 3145732
  43.1 2.2 copy-start.1
  74.7 4.6 %copy-start.3 = (s32[32,4]{0,1:T(4,128)S(1)}, s32[32,4]{0,1:T(4,128)}, u32[]{:S(2)}) copy-start(s32[32,4]{0,1:T(4,128)} %param.10) | copy-start | bytes 1540
  74.7 242.0 %all-to-all-start = ((bf16[32,8,128,128]{3,2,1,0:T(8,128)(2,1)}), bf16[32,8,128,128]{3,2,1,0:T(8,128)(2,1)}, u32[]{:S(2)}, u32[]{:S(2)}) async-start(bf16[32,8,128,128]{3,2,1,0:T(8,128)(2,1)} %scatter_fusion), calls=%async_computation | async-start | bytes 16777216 | tf_op jit(solution)/shard_map/all_to_all | solution.py:34
  78.6 189.9 %all-gather.3.cloned.1.call-start = ((), (), s32[]{:S(2)}) async-start(), calls=%async_computation.1 | async-start | bytes 5898240 | tf_op jit(solution)/shard_map/all_gather | solution.py:49
  316.7 10.5 %copy-start.2 = (s32[512]{0:T(512)S(1)}, s32[512]{0:T(512)}, u32[]{:S(2)}) copy-start(s32[512]{0:T(512)} %param.9) | copy-start | bytes 6148
Sparse Core Ops, SparseCore 0:
  81.2 113.6 all-gather.2
where the time goes:
time: 403 us; the launch traced here: 402 us
  blocking collectives  300 us (74%)
  local copies, waits for them, and re-layouts  41.4 us (10%)
  matrix products  34.7 us (9%)
  between operations  14.1 us (3%)
  other arithmetic  7.81 us (2%)
    all_gather x1, blocking collectives, local(): lax.all_gather(map_target, 'vocab', axis=0, tiled=True)  189 us
    psum x1, blocking collectives, local(): lax.psum((exp_part, mass_part, inner_part, label_part), ('tok', 'vocab'))  41.5 us
    pmax x1, blocking collectives, local(): top_all = lax.pmax(row_top, ('tok', 'vocab'))  38.1 us
    scatter x1, local copies, waits for them, and re-layouts, local(): jnp.zeros((nodes, capacity, tok_rows, block), jnp.bfloat16)  20.7 us
    pmax x1, blocking collectives, local(): highest = lax.pmax(local_top, 'vocab')  18.1 us
    unnamed x10, local copies, waits for them, and re-layouts  14.1 us
    psum x1, blocking collectives, local(): lax.psum(jnp.sum(jnp.exp(scores - highest[:, None]), axis=1), 'vocab')  13.6 us
    dot_general x1, matrix products, local(): lax.dot_general(everyone, grad_logits, (((0,), (0,)), ((), ())), preferre...  11 us
  transfers between devices with their start and end apart: 2, of which 0 were waited for; matrix products, arithmetic and copies ran while one was open for 3% of the time, Pallas kernels for 0%

commit v1 on v0

v1 whole, which is shorter than its diff:
```python
import functools

import jax
import jax.numpy as jnp
from jax import lax
from jax.experimental import pallas as pl
from jax.experimental.pallas import tpu as pltpu
from jax.sharding import PartitionSpec as P

F32 = jnp.float32
BF16 = jnp.bfloat16
LANES = 128
GROUP = 8
VMEM_LIMIT = 56 * 1024 * 1024


def rows_from_columns(columns):
    n = columns[0].shape[0]
    lane = lax.broadcasted_iota(jnp.int32, (n, LANES), 1)
    tile = jnp.zeros((n, LANES), F32)
    for place, column in enumerate(columns):
        tile = jnp.where(lane == place, column, tile)
    return tile.T[0:8, :]


def teacher_kernel(x_ref, stat_ref):
    rows, cols = x_ref.shape
    pieces = [x_ref[:, j : j + LANES].astype(F32) for j in range(0, cols, LANES)]
    top = jnp.max(functools.reduce(jnp.maximum, pieces), axis=1, keepdims=True)
    total = jnp.zeros((rows, LANES), F32)
    for j in range(0, cols, LANES):
        total = total + jnp.exp(x_ref[:, j : j + LANES].astype(F32) - top)
    stat_ref[...] = rows_from_columns([top, jnp.sum(total, axis=1, keepdims=True)])


def teacher_stats(x):
    vmem = pl.BlockSpec(memory_space=pltpu.VMEM)
    return pl.pallas_call(
        teacher_kernel,
        in_specs=[vmem],
        out_specs=vmem,
        out_shape=jax.ShapeDtypeStruct((8, x.shape[0]), F32),
        compiler_params=pltpu.CompilerParams(vmem_limit_bytes=VMEM_LIMIT),
        cost_estimate=pl.CostEstimate(flops=4 * x.size, bytes_accessed=2 * x.size, transcendentals=x.size),
        name="teacher_stats",
    )(x)


def contrib_kernel(
    core_ref, own_code, peer_code, stats_ref, x_own, x_peer, w_own, w_peer, out_ref, mass_ref, acc, probs, *, steps, fan
):
    chunk, step = pl.program_id(0), pl.program_id(1)
    blocks = x_own.shape[1] // LANES
    rows = x_own.shape[0]
    slots = out_ref.shape[0]

    @pl.when((chunk == 0) & (step == 0))
    def _():
        n_vocab = stats_ref.shape[0]
        row = lambda v, k: stats_ref[v, k : k + 1, :]
        top = functools.reduce(jnp.maximum, [row(v, 0) for v in range(n_vocab)])
        total = functools.reduce(jnp.add, [row(v, 1) * jnp.exp(row(v, 0) - top) for v in range(n_vocab)])
        columns = jnp.concatenate([top, total, jnp.zeros((LANES - 2, rows), F32)], axis=0).T
        top, total = columns[:, 0:1], columns[:, 1:2]
        for side, x in enumerate((x_own, x_peer)):
            for j in range(blocks):
                raised = jnp.exp(x[:, j * LANES : (j + 1) * LANES].astype(F32) - top)
                probs[side * blocks + j] = (raised / total).astype(BF16)

    @pl.when(step == 0)
    def _():
        acc[...] = jnp.zeros_like(acc)

    def add(code_ref, w_ref, first, offset):
        for jj in range(GROUP):
            piece = probs[offset + first + jj]
            for f in range(fan):
                code = code_ref[(first + jj) * fan + f]
                slot = lax.shift_right_logical(code, 1) - chunk * slots
                mine = ((code & 1) == core_ref[0]) & (slot >= 0) & (slot < slots)
                slot = jnp.where(mine, slot, slots)
                part = jnp.dot(piece, w_ref[jj, f], preferred_element_type=F32)
                acc[slot] += part.astype(BF16).astype(F32)

    @pl.when(step < steps)
    def _():
        add(own_code, w_own, step * GROUP, 0)

    @pl.when(step >= steps)
    def _():
        add(peer_code, w_peer, (step - steps) * GROUP, blocks)

    @pl.when(step == 2 * steps - 1)
    def _():
        def body(i, mass):
            block = acc[i]
            out_ref[i] = block.astype(BF16)
            return mass + block

        mass = lax.fori_loop(0, slots, body, jnp.zeros((rows, LANES), F32), unroll=4)
        mass = jnp.sum(mass, axis=1, keepdims=True)
        part = rows_from_columns([mass])

        @pl.when(chunk == 0)
        def _():
            mass_ref[...] = part

        @pl.when(chunk > 0)
        def _():
            mass_ref[...] += part


def contributions(core, own_code, peer_code, stats, x_own, x_peer, w_own, w_peer, slots_all, slots):
    rows = x_own.shape[0]
    old_blocks, fan = w_own.shape[:2]
    steps = old_blocks // GROUP
    chunks = slots_all // slots
    smem = pl.BlockSpec(memory_space=pltpu.SMEM)
    whole = lambda shape: pl.BlockSpec(shape, lambda c, s: (0,) * len(shape))
    weights = (GROUP, fan, LANES, LANES)
    return pl.pallas_call(
        functools.partial(contrib_kernel, steps=steps, fan=fan),
        grid=(chunks, 2 * steps),
        in_specs=[
            smem,
            smem,
            smem,
            whole(stats.shape),
            whole(x_own.shape),
            whole(x_peer.shape),
            pl.BlockSpec(weights, lambda c, s: (jnp.minimum(s, steps - 1), 0, 0, 0)),
            pl.BlockSpec(weights, lambda c, s: (jnp.maximum(s - steps, 0), 0, 0, 0)),
        ],
        out_specs=[
            pl.BlockSpec((slots, rows, LANES), lambda c, s: (c, 0, 0)),
            whole((8, rows)),
        ],
        out_shape=[
            jax.ShapeDtypeStruct((slots_all, rows, LANES), BF16),
            jax.ShapeDtypeStruct((8, rows), F32),
        ],
        scratch_shapes=[
            pltpu.VMEM((slots + 1, rows, LANES), F32),
            pltpu.VMEM((2 * old_blocks, rows, LANES), BF16),
        ],
        compiler_params=pltpu.CompilerParams(vmem_limit_bytes=VMEM_LIMIT),
        cost_estimate=pl.CostEstimate(
            flops=4 * old_blocks * fan * rows * LANES * LANES,
            bytes_accessed=2 * x_own.size * 2 + 2 * w_own.size * 2 + slots_all * rows * LANES * 2,
            transcendentals=2 * x_own.size,
        ),
        name="chip_sums",
    )(core, own_code, peer_code, stats, x_own, x_peer, w_own, w_peer)


def student_kernel(base_ref, logits_ref, labels_ref, mass_ref, stat_ref):
    n_tok, rows, cols = logits_ref.shape
    lane = lax.broadcasted_iota(jnp.int32, (rows, LANES), 1)
    label = labels_ref[...]
    top = jnp.full((rows, LANES), -jnp.inf, F32)
    hit = jnp.zeros((rows, LANES), F32)
    for t in range(n_tok):
        for b in range(cols // LANES):
            block = logits_ref[t, :, b * LANES : (b + 1) * LANES]
            top = jnp.maximum(top, block)
            hit = hit + jnp.where(lane == label - (base_ref[t] + b * LANES), block, 0.0)
    top = jnp.max(top, axis=1, keepdims=True)
    total = jnp.zeros((rows, LANES), F32)
    for t in range(n_tok):
        for b in range(cols // LANES):
            total = total + jnp.exp(logits_ref[t, :, b * LANES : (b + 1) * LANES] - top)
    total = jnp.sum(total, axis=1, keepdims=True)
    hit = jnp.sum(hit, axis=1, keepdims=True)
    zero = jnp.zeros_like(hit)
    stat_ref[...] = mass_ref[...] + rows_from_columns([zero, top, total, hit])


def student_stats(base, logits, label_column, mass):
    smem = pl.BlockSpec(memory_space=pltpu.SMEM)
    vmem = pl.BlockSpec(memory_space=pltpu.VMEM)
    return pl.pallas_call(
        student_kernel,
        in_specs=[smem, vmem, vmem, vmem],
        out_specs=vmem,
        out_shape=jax.ShapeDtypeStruct(mass.shape, F32),
        compiler_params=pltpu.CompilerParams(vmem_limit_bytes=VMEM_LIMIT),
        cost_estimate=pl.CostEstimate(
            flops=4 * logits.size, bytes_accessed=4 * logits.size, transcendentals=logits.size
        ),
        name="student_stats",
    )(base, logits, label_column, mass)


def grad_kernel(base_ref, stats_ref, sums_ref, logits_ref, labels_ref, grad_ref, loss_ref, columns, inner):
    t = pl.program_id(0)
    n_vocab = stats_ref.shape[0]
    n_z, per, rows, _ = sums_ref.shape

    @pl.when(t == 0)
    def _():
        row = lambda v, k: stats_ref[v, k : k + 1, :]
        mass = functools.reduce(jnp.add, [row(v, 0) for v in range(n_vocab)])
        high = functools.reduce(jnp.maximum, [row(v, 1) for v in range(n_vocab)])
        spread = functools.reduce(jnp.add, [row(v, 2) * jnp.exp(row(v, 1) - high) for v in range(n_vocab)])
        log_total = high + jnp.log(spread)
        label_logit = functools.reduce(jnp.add, [row(v, 3) for v in range(n_vocab)])
        head = [mass + 1.0, log_total]
        fill = jnp.zeros((LANES - len(head), rows), F32)
        columns[...] = jnp.concatenate(head + [fill], axis=0).T
        inner[...] = jnp.zeros_like(inner)
        loss_ref[0:1, :] = mass * log_total + log_total - label_logit

    lane = lax.broadcasted_iota(jnp.int32, (rows, LANES), 1)
    label = labels_ref[...] - base_ref[t]
    lift = columns[:, 0:1]
    log_total = columns[:, 1:2]
    running = inner[...]
    for b in range(per):
        target = sums_ref[0, b].astype(F32)
        for z in range(1, n_z):
            target = target + sums_ref[z, b].astype(F32)
        logits = logits_ref[0, :, b * LANES : (b + 1) * LANES]
        running = running + target * logits
        hit = jnp.where(lane == label - b * LANES, 1.0, 0.0)
        grad = lift * jnp.exp(logits - log_total) - target - hit
        grad_ref[0, :, b * LANES : (b + 1) * LANES] = grad.astype(BF16)
    inner[...] = running

    @pl.when(t == pl.num_programs(0) - 1)
    def _():
        part = jnp.sum(inner[...], axis=1, keepdims=True)
        loss_ref[1:2, :] = rows_from_columns([part])[0:1, :]


def grad_logits(base, stats, sums, logits, label_column):
    n_tok, rows, cols = logits.shape
    n_z, slots = sums.shape[:2]
    per = slots // n_tok
    smem = pl.BlockSpec(memory_space=pltpu.SMEM)
    return pl.pallas_call(
        grad_kernel,
        grid=(n_tok,),
        in_specs=[
            smem,
            pl.BlockSpec(stats.shape, lambda t: (0, 0, 0)),
            pl.BlockSpec((n_z, per, rows, LANES), lambda t: (0, t, 0, 0)),
            pl.BlockSpec((1, rows, cols), lambda t: (t, 0, 0)),
            pl.BlockSpec((rows, 1), lambda t: (0, 0)),
        ],
        out_specs=[
            pl.BlockSpec((1, rows, cols), lambda t: (t, 0, 0)),
            pl.BlockSpec((8, rows), lambda t: (0, 0)),
        ],
        out_shape=[
            jax.ShapeDtypeStruct((n_tok, rows, cols), BF16),
            jax.ShapeDtypeStruct((8, rows), F32),
        ],
        scratch_shapes=[pltpu.VMEM((rows, LANES), F32), pltpu.VMEM((rows, LANES), F32)],
        compiler_params=pltpu.CompilerParams(vmem_limit_bytes=VMEM_LIMIT),
        cost_estimate=pl.CostEstimate(
            flops=16 * logits.size, bytes_accessed=2 * sums.size + 6 * logits.size, transcendentals=logits.size
        ),
        name="grad_logits",
    )(base, stats, sums, logits, label_column)


def matmul_kernel(a_ref, b_ref, o_ref):
    o_ref[...] = jnp.dot(a_ref[...], b_ref[...], preferred_element_type=F32).astype(o_ref.dtype)


def head_product(a, b):
    m, k = a.shape
    n = b.shape[1]
    tile = 512
    while m % tile:
        tile //= 2
    return pl.pallas_call(
        matmul_kernel,
        grid=(m // tile,),
        in_specs=[
            pl.BlockSpec((tile, k), lambda i: (i, 0)),
            pl.BlockSpec((k, n), lambda i: (0, 0)),
        ],
        out_specs=pl.BlockSpec((tile, n), lambda i: (i, 0)),
        out_shape=jax.ShapeDtypeStruct((m, n), BF16),
        compiler_params=pltpu.CompilerParams(vmem_limit_bytes=VMEM_LIMIT),
        cost_estimate=pl.CostEstimate(
            flops=2 * m * n * k, bytes_accessed=2 * (m * k + k * n + m * n), transcendentals=0
        ),
        name="head_product",
    )(a, b)


def local(teacher_logits, hidden, new_head, labels, map_target, map_weight):
    rows = teacher_logits.shape[0]
    block = map_weight.shape[2]
    n_tok = lax.axis_size("tok")
    n_vocab = lax.axis_size("vocab")
    n_z = n_vocab // 2
    new_cols = new_head.shape[1]
    per = new_cols // block
    tok = lax.axis_index("tok")
    vocab = lax.axis_index("vocab")
    slots = n_tok * per
    slots_all = n_z * slots

    everyone = lax.all_gather(hidden, "tok", axis=0, tiled=True)

    owner = map_target // per
    owner_vocab = owner % n_vocab
    slot = (owner_vocab // 2) * slots + (owner // n_vocab) * per + map_target % per
    own_code = (slot * 2 + owner_vocab % 2).astype(jnp.int32).reshape(-1)
    swap = [(v, v ^ 1) for v in range(n_vocab)]
    peer_logits = lax.ppermute(teacher_logits, "vocab", swap)
    peer_code = lax.ppermute(own_code, "vocab", swap)
    peer_weight = lax.ppermute(map_weight, "vocab", swap)
    core = (vocab % 2).astype(jnp.int32).reshape(1)
    at_once = min(slots_all, 128)
    totals = lax.all_gather(teacher_stats(teacher_logits), "vocab", axis=0)
    sums, mass = contributions(
        core, own_code, peer_code, totals, teacher_logits, peer_logits, map_weight, peer_weight, slots_all, at_once
    )

    sums = sums.reshape(n_z, slots, rows, block)
    lines = [[2 * z + c for z in range(n_z)] for c in range(2)]
    sums = lax.all_to_all(sums, "vocab", split_axis=0, concat_axis=0, axis_index_groups=lines, tiled=True)

    logits = jnp.dot(everyone, new_head, preferred_element_type=F32)
    turned = everyone.T
    logits = lax.all_to_all(
        logits.reshape(n_tok, rows, new_cols), "tok", split_axis=0, concat_axis=0, tiled=True
    )
    label_column = lax.dynamic_slice_in_dim(labels, tok * rows, rows).reshape(rows, 1)
    base = (jnp.arange(n_tok, dtype=jnp.int32) * n_vocab + vocab) * new_cols
    stats = student_stats(base, logits, label_column, mass)
    stats = lax.all_gather(stats, "vocab", axis=0)

    grad, loss_rows = grad_logits(base, stats, sums, logits, label_column)
    grad = lax.all_to_all(grad, "tok", split_axis=0, concat_axis=0, tiled=True)
    inner = lax.psum(loss_rows[1], "vocab")
    loss = loss_rows[0] - inner
    head_grad = head_product(turned, grad.reshape(n_tok * rows, new_cols))
    return (loss, head_grad)


def solution(mesh):
    return jax.shard_map(
        local,
        mesh=mesh,
        in_specs=(
            P("tok", "vocab"),
            P("tok", None),
            P(None, ("tok", "vocab")),
            P(),
            P("vocab", None),
            P("vocab", None, None, None),
        ),
        out_specs=(P("tok"), P(None, ("tok", "vocab"))),
        check_vma=False,
    )
```

time: 403 us -> 269 us (0.67)
  blocking collectives: 300 us -> 127 us
  waiting for transfers between devices: 0.7 us -> 59.9 us
  local copies, waits for them, and re-layouts: 41.4 us -> 5.57 us
  Pallas kernels: 0 us -> 35.1 us
  matrix products: 34.7 us -> 10.1 us
  starting transfers between devices: 3.85 us -> 13.7 us
  other arithmetic: 7.81 us -> 1.73 us
    all_gather x1 -> x2, blocking collectives: 189 us -> 112 us  [the longest x1 96.8 us: local(): stats = lax.all_gather(stats, 'vocab', axis=0)]
    all_gather x1, waiting for transfers between devices: 0.02 us -> 59.9 us  [local(): everyone = lax.all_gather(hidden, 'tok', axis=0, tiled=True)]
    pmax x2 -> x0, blocking collectives: 56.2 us -> none  [the longest x1 38.1 us: local(): top_all = lax.pmax(row_top, ('tok', 'vocab'))]
    psum x2 -> x1, blocking collectives: 55.1 us -> 15.5 us  [local(): inner = lax.psum(loss_rows[1], 'vocab')]
    pallas_call x0 -> x5, Pallas kernels: none -> 35.1 us  [the longest x1 12.7 us: contributions(): pl.pallas_call(functools.partial(contrib_kernel, steps=steps, fan=fan), g...]
    dot_general x4 -> x1, matrix products: 34.7 us -> 10.1 us  [local(): logits = jnp.dot(everyone, new_head, preferred_element_type=F32)]
    scatter x1 -> x0, local copies, waits for them, and re-layouts: 20.7 us -> none  [local(): jnp.zeros((nodes, capacity, tok_rows, block), jnp.bfloat16)]
    unnamed x10 -> x15, local copies, waits for them, and re-layouts: 14.1 us -> 3.88 us
  transfers between devices with their start and end apart: 2 -> 7, of which waited for: 0 -> 1; matrix products, arithmetic and copies ran while one was open for 3% -> 5% of each run, Pallas kernels for 0% -> 7%
where the time goes in v1:
time: 269 us; the launch traced here: 268 us
  blocking collectives  127 us (47%)
  waiting for transfers between devices  59.9 us (22%)
  Pallas kernels  35.1 us (13%)
  between operations  14.2 us (5%)
  starting transfers between devices  13.7 us (5%)
  matrix products  10.1 us (4%)
  local copies, waits for them, and re-layouts  5.57 us (2%)
    all_gather x1, blocking collectives, local(): stats = lax.all_gather(stats, 'vocab', axis=0)  96.8 us
    all_gather x1, waiting for transfers between devices, local(): everyone = lax.all_gather(hidden, 'tok', axis=0, tiled=True)  59.9 us
    psum x1, blocking collectives, local(): inner = lax.psum(loss_rows[1], 'vocab')  15.5 us
    all_gather x1, blocking collectives, local(): totals = lax.all_gather(teacher_stats(teacher_logits), 'vocab', axis=0)  14.9 us
    pallas_call x1, Pallas kernels, contributions(): pl.pallas_call(functools.partial(contrib_kernel, steps=steps, fan=fan), g...  12.7 us
    pallas_call x1, Pallas kernels, head_product(): pl.pallas_call(matmul_kernel, grid=(m // tile,), in_specs=[pl.BlockSpec((...  11.7 us
    dot_general x1, matrix products, local(): logits = jnp.dot(everyone, new_head, preferred_element_type=F32)  10.1 us
  transfers between devices with their start and end apart: 7, of which 1 were waited for; matrix products, arithmetic and copies ran while one was open for 5% of the time, Pallas kernels for 7%

profile of v1, /device:TPU:0, one launch (start us, length us, event | category | flops | bytes accessed | tf_op | source)
XLA Modules:
  0.0 267.6 jit_solution(3132273644131284618)
XLA Ops:
  7.2 0.0 copy-start
  7.2 0.0 all-gather.4.cloned.1.call-start
  7.2 2.4 copy.12
  9.6 0.0 all-gather.4.cloned.1.call-update
  9.6 0.0 copy-start.2
  9.6 0.0 copy-start.5
  9.6 0.5 collective-permute-start.2
  10.2 59.9 %all-gather.4.cloned.1.call-done = bf16[512,4608]{0,1:T(8,128)(2,1)} async-done(((bf16[128,4608]{0,1:T(8,128)(2,1)}), bf16[512,4608]{0,1:T(8,128)(2,1)}) %all-gather.4.cloned.1.call-update) | async-done | bytes 4718608 | tf_op jit(solution)/shard_map/all_gather | solution.py:307
  70.1 10.1 %fusion.11 = f32[512,1024]{1,0:T(8,128)} fusion(bf16[512,4608]{0,1:T(8,128)(2,1)} %all-gather.4.cloned.1.call-done, bf16[4608,1024]{1,0:T(8,128)(2,1)} %param.8), kind=kOutput, calls=%fused_computation.33 | convolution fusion | flops 4831838208 | bytes 16252928 | tf_op jit(solution)/shard_map/dot_general | solution.py:328
  80.2 3.6 %all-to-all-start = ((f32[4,128,1024]{2,1,0:T(8,128)}), f32[4,128,1024]{2,1,0:T(8,128)S(1)}, u32[]{:S(2)}, u32[]{:S(2)}) async-start(f32[4,128,1024]{2,1,0:T(8,128)} %bitcast.16), calls=%async_computation | async-start | bytes 4194304 | tf_op jit(solution)/shard_map/all_to_all | solution.py:330
  83.8 0.1 collective-permute-start.1
  83.9 0.1 copy.13
  84.0 0.1 reshape.25.own_code
  84.1 0.6 collective-permute-start
  84.7 2.4 teacher_stats.1
  87.1 14.9 %all-gather = f32[64,128]{1,0:T(8,128)} all-gather(f32[8,128]{1,0:T(8,128)} %teacher_stats.1), channel_id=2, replica_groups=mesh['tok'=4,'vocab'=8] {'vocab'}, dimensions={0}, use_global_device_ids=true | all-gather | bytes 36864 | tf_op jit(solution)/shard_map/all_gather | solution.py:319
  102.0 0.0 collective-permute-done.2.w_peer
  102.0 0.5 copy-done.6
  102.5 12.7 %chip_sums.1 = (bf16[128,128,128]{2,1,0:T(8,128)(2,1)}, f32[8,128]{1,0:T(8,128)}) custom-call(s32[1]{0:T(128)} %bitcast.2.core_ref, s32[128]{0:T(128)} %copy-done.4, s32[128]{0:T(128)} %copy-done.6, f32[8,8,128]{2,1,0:T(8,128)} %bitcast.18, bf16[128,4096]{1,0:T(8,128)(2,1)} %x_own.1, bf16[128,4096]{1,0:T(8,128)(2,1)} %collective-permute-done.1.x_peer, ...), custom_call_target="tpu_custom_call" | custom-call | flops 1073741824 | bytes 14680064 | tf_op jit(solution)/shard_map/chip_sums/pallas_call | solution.py:121
  115.2 4.9 %all-to-all-start.1 = ((bf16[4,32,128,128]{3,2,1,0:T(8,128)(2,1)}), bf16[4,32,128,128]{3,2,1,0:T(8,128)(2,1)}, u32[]{:S(2)}, u32[]{:S(2)}) async-start(bf16[4,32,128,128]{3,2,1,0:T(8,128)(2,1)} %bitcast.15), calls=%async_computation.1 | async-start | bytes 8388608 | tf_op jit(solution)/shard_map/all_to_all | solution.py:326
  120.1 0.1 dynamic-slice_bitcast_fusion
  120.2 0.7 copy.14.labels_ref
  120.9 0.5 add_multiply_fusion.base_ref
  121.4 3.1 %student_stats.1 = f32[8,128]{1,0:T(8,128)} custom-call(s32[4]{0:T(128)} %add_multiply_fusion.base_ref, f32[4,128,1024]{2,1,0:T(8,128)} %copy-done.1, s32[128,1]{1,0:T(8,128)} %copy.14.labels_ref, f32[8,128]{1,0:T(8,128)} %get-tuple-element.6.mass_ref), custom_call_target="tpu_custom_call" | custom-call | flops 2097152 | bytes 2097152 | tf_op jit(solution)/shard_map/student_stats/pallas_call | solution.py:181
  124.5 96.8 %all-gather.1 = f32[64,128]{1,0:T(8,128)} all-gather(f32[8,128]{1,0:T(8,128)} %student_stats.1), channel_id=3, replica_groups=mesh['tok'=4,'vocab'=8] {'vocab'}, dimensions={0}, use_global_device_ids=true | all-gather | bytes 36864 | tf_op jit(solution)/shard_map/all_gather | solution.py:336
  221.3 5.3 %grad_logits.1 = (bf16[4,128,1024]{2,1,0:T(8,128)(2,1)}, f32[8,128]{1,0:T(8,128)}) custom-call(s32[4]{0:T(128)} %add_multiply_fusion.base_ref, f32[8,8,128]{2,1,0:T(8,128)} %bitcast.19, bf16[4,32,128,128]{3,2,1,0:T(8,128)(2,1)} %all-to-all-done.1.sums_ref, f32[4,128,1024]{2,1,0:T(8,128)} %copy-done.1, s32[128,1]{1,0:T(8,128)} %copy.14.labels_ref), custom_call_target="tpu_custom_call" | custom-call | flops 8388608 | bytes 7340032 | tf_op jit(solution)/shard_map/grad_logits/pallas_call | solution.py:240
  226.6 4.1 %all-to-all-start.2 = ((bf16[4,128,1024]{2,1,0:T(8,128)(2,1)}), bf16[4,128,1024]{2,1,0:T(8,128)(2,1)S(1)}, u32[]{:S(2)}, u32[]{:S(2)}) async-start(bf16[4,128,1024]{2,1,0:T(8,128)(2,1)} %get-tuple-element.9), calls=%async_computation.2 | async-start | bytes 2097152 | tf_op jit(solution)/shard_map/all_to_all | solution.py:339
  230.7 0.7 slice_bitcast_fusion
  231.3 15.5 %psum.7 = f32[128]{0:T(128)S(1)} all-reduce(f32[128]{0:T(128)S(1)} %slice_bitcast_fusion), channel_id=1, replica_groups=mesh['tok'=4,'vocab'=8] {'vocab'}, use_global_device_ids=true, to_apply=%region_0.1 | all-reduce | flops 128 | bytes 1024 | tf_op jit(solution)/shard_map/psum | solution.py:340
  246.9 1.2 bitcast_subtract_fusion
  248.1 1.0 copy-done.3
  249.1 11.7 %head_product.1 = bf16[4608,1024]{1,0:T(8,128)(2,1)} custom-call(bf16[4608,512]{1,0:T(8,128)(2,1)} %bitcast.20, bf16[512,1024]{1,0:T(8,128)(2,1)} %bitcast.17), custom_call_target="tpu_custom_call" | custom-call | flops 4831838208 | bytes 15204352 | tf_op jit(solution)/shard_map/head_product/pallas_call | solution.py:277
  (15 shorter events, 0.1 us)
Async XLA Ops:
  7.2 112.9 %copy-start = (s32[512]{0:T(512)S(1)}, s32[512]{0:T(512)}, u32[]{:S(2)}) copy-start(s32[512]{0:T(512)} %param.9) | copy-start | bytes 6148
  7.2 62.9 %all-gather.4.cloned.1.call-start = ((), (), s32[]{:S(2)}) async-start(), calls=%async_computation.3 | async-start | bytes 5898240 | tf_op jit(solution)/shard_map/all_gather | solution.py:307
  9.6 74.1 %copy-start.2 = (bf16[128,4096]{1,0:T(8,128)(2,1)S(1)}, bf16[128,4096]{1,0:T(8,128)(2,1)}, u32[]{:S(2)}) copy-start(bf16[128,4096]{1,0:T(8,128)(2,1)} %x_own.1) | copy-start | bytes 3145732
  9.6 74.2 %copy-start.5 = (s32[32,4]{0,1:T(4,128)S(1)}, s32[32,4]{0,1:T(4,128)}, u32[]{:S(2)}) copy-start(s32[32,4]{0,1:T(4,128)} %param.10) | copy-start | bytes 1540
  9.6 92.4 %collective-permute-start.2 = (bf16[32,4,128,128]{3,2,1,0:T(8,128)(2,1)}, bf16[32,4,128,128]{3,2,1,0:T(8,128)(2,1)}, u32[]{:S(2)}, u32[]{:S(2)}) collective-permute-start(bf16[32,4,128,128]{3,2,1,0:T(8,128)(2,1)} %w_own.1), channel_id=1, source_target_pairs={{0,1},{1,0},{2,3},{3,2},{4,5},{5,4},{6,7},{7,6},{8,9},{9,8},{10,11... | collective-permute-start | bytes 12582920 | tf_op jit(solution)/shard_map/ppermute | solution.py:316
  80.2 35.0 %all-to-all-start = ((f32[4,128,1024]{2,1,0:T(8,128)}), f32[4,128,1024]{2,1,0:T(8,128)S(1)}, u32[]{:S(2)}, u32[]{:S(2)}) async-start(f32[4,128,1024]{2,1,0:T(8,128)} %bitcast.16), calls=%async_computation | async-start | bytes 4194304 | tf_op jit(solution)/shard_map/all_to_all | solution.py:330
  83.8 18.2 %collective-permute-start.1 = (bf16[128,4096]{1,0:T(8,128)(2,1)S(1)}, bf16[128,4096]{1,0:T(8,128)(2,1)}, u32[]{:S(2)}, u32[]{:S(2)}) collective-permute-start(bf16[128,4096]{1,0:T(8,128)(2,1)S(1)} %copy-done.2), channel_id=1, source_target_pairs={{0,1},{1,0},{2,3},{3,2},{4,5},{5,4},{6,7},{7,6},{8,9},{9,8},{10,11... | collective-permute-start | bytes 3145736 | tf_op jit(solution)/shard_map/ppermute | solution.py:314
  84.1 17.9 %copy-start.4 = (s32[128]{0:T(128)}, s32[128]{0:T(128)S(1)}, u32[]{:S(2)}) copy-start(s32[128]{0:T(128)S(1)} %reshape.25.own_code) | copy-start | bytes 1540
  84.1 17.9 %collective-permute-start = (s32[128]{0:T(128)S(1)}, s32[128]{0:T(128)S(1)}, u32[]{:S(2)}, u32[]{:S(2)}) collective-permute-start(s32[128]{0:T(128)S(1)} %reshape.25.own_code), channel_id=1, source_target_pairs={{0,1},{1,0},{2,3},{3,2},{4,5},{5,4},{6,7},{7,6},{8,9},{9,8},{10,11... | collective-permute-start | bytes 1544 | tf_op jit(solution)/shard_map/ppermute | solution.py:315
  102.0 0.5 copy-start.6
  115.2 6.2 %copy-start.1 = (f32[4,128,1024]{2,1,0:T(8,128)}, f32[4,128,1024]{2,1,0:T(8,128)S(1)}, u32[]{:S(2)}) copy-start(f32[4,128,1024]{2,1,0:T(8,128)S(1)} %all-to-all-done.logits_ref) | copy-start | bytes 6291460
  115.2 106.1 %all-to-all-start.1 = ((bf16[4,32,128,128]{3,2,1,0:T(8,128)(2,1)}), bf16[4,32,128,128]{3,2,1,0:T(8,128)(2,1)}, u32[]{:S(2)}, u32[]{:S(2)}) async-start(bf16[4,32,128,128]{3,2,1,0:T(8,128)(2,1)} %bitcast.15), calls=%async_computation.1 | async-start | bytes 8388608 | tf_op jit(solution)/shard_map/all_to_all | solution.py:326
  226.6 21.5 %all-to-all-start.2 = ((bf16[4,128,1024]{2,1,0:T(8,128)(2,1)}), bf16[4,128,1024]{2,1,0:T(8,128)(2,1)S(1)}, u32[]{:S(2)}, u32[]{:S(2)}) async-start(bf16[4,128,1024]{2,1,0:T(8,128)(2,1)} %get-tuple-element.9), calls=%async_computation.2 | async-start | bytes 2097152 | tf_op jit(solution)/shard_map/all_to_all | solution.py:339
  248.1 1.0 copy-start.3
Sparse Core Ops, SparseCore 0:
  10.4 59.6 all-gather.3
